TPU v7x, 32 devices: a whole 2x2x4 slice. The times are simulated.
32 devices in a mesh: row: 8 (over y, x, core), col: 4 (over z).
Axes of the slice: x: 2, y: 2, z: 4, core: 2. Of those that a mesh axis runs over, the one named last changes fastest.
Arguments:
- covariance: float32 [2048, 2048], P('row', 'col'), may hold values from -5 to 60, as said below
- dynamics: float32 [16, 5, 128, 128], P('row', None, 'col'), may hold values from -0.25 to 0.25
- noise_factor: float32 [16, 128, 128], P('row', 'col'), may hold values from -4 to 4
Outputs:
- forecast: float32 [2048, 2048], P('row', 'col')
Inputs may be any that keep to these rules, and one draw needn't show every extreme that they name: covariance is symmetric.
All inputs are finite; a program needn't handle non-finite values.
Results may differ from a plain program's by a relative error of at most 0.00012.
Values sent between devices are 32-bit elements; how exact they have to be, the bound alone decides.
A program may use at most 64 MiB of HBM per device.

v0:
```python
import jax
import jax.numpy as jnp
from jax import lax
from jax.sharding import PartitionSpec as P

STEPS = 2


def from_root(block, axis, owner):
    block = jnp.where(lax.axis_index(axis) == owner, block, jnp.zeros_like(block))
    return lax.psum(block, axis)


def extended_2(array, sides, width):
    for axis, dim in sides:
        peers, length = (lax.axis_size(axis), array.shape[dim])
        up = [(i, (i + 1) % peers) for i in range(peers - 1)]
        down = [(j, i) for i, j in up]
        last = lax.slice_in_dim(array, length - width, length, axis=dim)
        leading = lax.slice_in_dim(array, 0, width, axis=dim)
        before = lax.ppermute(last, axis, up)
        after = lax.ppermute(leading, axis, down)
        array = jnp.concatenate([before, array, after], axis=dim)
    return array


def rows_product(extended, dyn_rows, rows, band):
    local_bands = dyn_rows.shape[0]
    width = extended.shape[1]
    total = jnp.zeros((local_bands, band, width), jnp.float32)
    for offset in range(5):
        window = extended[offset * band : offset * band + rows].reshape(local_bands, band, width)
        total = total + jnp.einsum(
            "kab,kbw->kaw", dyn_rows[:, offset], window, precision=lax.Precision.HIGHEST
        )
    return total.reshape(rows, width)


def cols_product(extended, dyn_cols, cols, band):
    rows = extended.shape[0]
    col_bands = dyn_cols.shape[0]
    total = jnp.zeros((rows, col_bands, band), jnp.float32)
    for offset in range(5):
        window = extended[:, offset * band : offset * band + cols].reshape(rows, col_bands, band)
        total = total + jnp.einsum(
            "rjb,jab->rja", window, dyn_cols[:, offset], precision=lax.Precision.HIGHEST
        )
    return total.reshape(rows, cols)


def body(covariance, dynamics, noise_factor):
    band = dynamics.shape[3]
    rows, cols = covariance.shape
    ratio = lax.axis_size("row") // lax.axis_size("col")
    col_index = lax.axis_index("col")
    row_index = lax.axis_index("row")
    dyn_rows, noise_full = (
        lax.all_gather(dynamics, "col", axis=2, tiled=True),
        lax.all_gather(noise_factor, "col", axis=1, tiled=True),
    )
    local_bands = dyn_rows.shape[0]
    pieces = []
    for member in range(ratio):
        pieces.append(from_root(dyn_rows, "row", col_index * ratio + member))
    dyn_cols = jnp.concatenate(pieces, 0)
    noise = 0.5 * (noise_full + jnp.swapaxes(noise_full, 1, 2))
    state = covariance
    for step in range(STEPS):
        extended = extended_2(state, (("row", 0),), 2 * band)
        first = rows_product(extended, dyn_rows, rows, band)
        margin = extended_2(first, (("col", 1),), 2 * band)
        result = cols_product(margin, dyn_cols, cols, band)
        for local in range(local_bands):
            global_band = row_index * local_bands + local
            start = global_band * band - col_index * cols
            inside = jnp.logical_and(start >= 0, start < cols)
            safe = jnp.clip(start, 0, cols - band)
            current = lax.dynamic_slice(result, (jnp.int32(local * band), safe), (band, band))
            updated = current + jnp.where(inside, noise[local], 0.0)
            result = lax.dynamic_update_slice(result, updated, (jnp.int32(local * band), safe))
        state = result
    return state


def solution(mesh):
    in_specs = (P("row", "col"), P("row", None, "col", None), P("row", "col", None))
    out_specs = P("row", "col")
    return jax.shard_map(body, mesh=mesh, in_specs=in_specs, out_specs=out_specs, check_vma=False)
```

profile of v0, /device:TPU:18, one launch (start us, length us, event | category | flops | bytes accessed | tf_op | source)
XLA Modules:
  0.0 146.6 jit_solution(3171462295319281378)
XLA Ops:
  6.5 1.9 %collective-permute-start = (f32[256,512]{1,0:T(8,128)}, f32[256,512]{1,0:T(8,128)S(1)}, u32[]{:S(2)}, u32[]{:S(2)}) collective-permute-start(f32[256,512]{1,0:T(8,128)} %param.3), channel_id=1, source_target_pairs={{0,4},{4,8},{8,12},{12,16},{16,20},{20,24},{24,28},{1,5},{5,9},{9,... | collective-permute-start | bytes 1572872 | tf_op jit(solution)/shard_map/ppermute | solution.py:21
  8.5 3.6 %collective-permute-start.1 = (f32[256,512]{1,0:T(8,128)}, f32[256,512]{1,0:T(8,128)S(1)}, u32[]{:S(2)}, u32[]{:S(2)}) collective-permute-start(f32[256,512]{1,0:T(8,128)} %param.3), channel_id=1, source_target_pairs={{4,0},{8,4},{12,8},{16,12},{20,16},{24,20},{28,24},{5,1},{9,5},{13... | collective-permute-start | bytes 1572872 | tf_op jit(solution)/shard_map/ppermute | solution.py:22
  12.1 0.9 copy.38
  13.0 16.4 %all_gather.6 = f32[2,5,128,128]{3,2,0,1:T(8,128)S(1)} all-gather(f32[2,5,32,128]{3,2,0,1:T(8,128)S(1)} %copy.38), channel_id=1, replica_groups=mesh['row'=8,'col'=4] {'col'}, dimensions={2}, use_global_device_ids=true | all-gather | bytes 819200 | tf_op jit(solution)/shard_map/all_gather | solution.py:58
  29.4 1.2 broadcast_select_fusion
  30.7 13.3 %all_gather.7 = f32[2,128,128]{2,0,1:T(2,128)S(1)} all-gather(f32[2,32,128]{2,0,1:T(2,128)S(1)} %copy.49), channel_id=1, replica_groups=mesh['row'=8,'col'=4] {'col'}, dimensions={1}, use_global_device_ids=true | all-gather | bytes 163840 | tf_op jit(solution)/shard_map/all_gather | solution.py:59
  46.2 0.6 fusion.4
  46.8 0.6 fusion.1
  47.6 0.8 fusion.20
  48.4 4.5 %collective-permute-start.2 = (f32[256,256]{0,1:T(8,128)}, f32[256,256]{0,1:T(8,128)S(1)}, u32[]{:S(2)}, u32[]{:S(2)}) collective-permute-start(f32[256,256]{0,1:T(8,128)} %get-tuple-element.26), channel_id=1, source_target_pairs={{0,1},{1,2},{2,3},{4,5},{5,6},{6,7},{8,9},{9,10},{10,11},{12,13},{... | collective-permute-start | bytes 786440 | tf_op jit(solution)/shard_map/ppermute | solution.py:21
  52.9 1.9 %collective-permute-start.3 = (f32[256,256]{0,1:T(8,128)}, f32[256,256]{0,1:T(8,128)}, u32[]{:S(2)}, u32[]{:S(2)}) collective-permute-start(f32[256,256]{0,1:T(8,128)} %get-tuple-element.25), channel_id=1, source_target_pairs={{1,0},{2,1},{3,2},{5,4},{6,5},{7,6},{9,8},{10,9},{11,10},{13,12},{... | collective-permute-start | bytes 786440 | tf_op jit(solution)/shard_map/ppermute | solution.py:22
  55.2 34.0 %all-reduce.3.cloned.1.call-done = (f32[2,5,128,128]{3,2,0,1:T(8,128)}, f32[2,5,128,128]{3,2,0,1:T(8,128)}) async-done(((f32[2,5,128,128]{3,2,0,1:T(8,128)}, f32[2,5,128,128]{3,2,0,1:T(8,128)}), (f32[2,5,128,128]{3,2,0,1:T(8,128)}, f32[2,5,128,128]{3,2,0,1:T(8,128)})) %all-reduce.3.cloned.1.call-update) | async-done | bytes 1310736 | tf_op jit(solution)/shard_map/psum | solution.py:11
  89.3 1.2 constant_dynamic-update-slice_fusion.1
  90.6 1.2 pad_maximum_fusion.4
  93.0 0.6 convolution_add_fusion.8
  95.1 1.7 %dynamic_update_slice.12 = f32[256,512]{1,0:T(8,128)S(1)} dynamic-update-slice(f32[256,512]{1,0:T(8,128)S(1)} %copy.52, f32[128,128]{1,0:T(8,128)S(1)} %bitcast_add_fusion.2, s32[]{:T(128)} %constant.24.clone.1, s32[]{:T(128)S(6)} %min.9) | dynamic-update-slice | bytes 131076 | tf_op jit(solution)/shard_map/dynamic_update_slice | solution.py:80
  96.9 1.1 dynamic_update_slice.13
  98.1 1.9 %collective-permute-start.4 = (f32[256,512]{1,0:T(8,128)S(1)}, f32[256,512]{1,0:T(8,128)S(1)}, u32[]{:S(2)}, u32[]{:S(2)}) collective-permute-start(f32[256,512]{1,0:T(8,128)S(1)} %dynamic_update_slice.13), channel_id=1, source_target_pairs={{0,4},{4,8},{8,12},{12,16},{16,20},{20,24},{24,28},{1,5},{5,9},{9,... | collective-permute-start | bytes 1572872 | tf_op jit(solution)/shard_map/ppermute | solution.py:21
  100.0 3.8 %collective-permute-start.5 = (f32[256,512]{1,0:T(8,128)S(1)}, f32[256,512]{1,0:T(8,128)S(1)}, u32[]{:S(2)}, u32[]{:S(2)}) collective-permute-start(f32[256,512]{1,0:T(8,128)S(1)} %dynamic_update_slice.13), channel_id=1, source_target_pairs={{4,0},{8,4},{12,8},{16,12},{20,16},{24,20},{28,24},{5,1},{9,5},{13... | collective-permute-start | bytes 1572872 | tf_op jit(solution)/shard_map/ppermute | solution.py:22
  104.4 4.1 %collective-permute-done.4 = f32[256,512]{1,0:T(8,128)S(1)} collective-permute-done((f32[256,512]{1,0:T(8,128)S(1)}, f32[256,512]{1,0:T(8,128)S(1)}, u32[]{:S(2)}, u32[]{:S(2)}) %collective-permute-start.4) | collective-permute-done | bytes 524320 | tf_op jit(solution)/shard_map/ppermute | solution.py:21
  108.6 4.6 %collective-permute-done.5 = f32[256,512]{1,0:T(8,128)S(1)} collective-permute-done((f32[256,512]{1,0:T(8,128)S(1)}, f32[256,512]{1,0:T(8,128)S(1)}, u32[]{:S(2)}, u32[]{:S(2)}) %collective-permute-start.5) | collective-permute-done | bytes 524320 | tf_op jit(solution)/shard_map/ppermute | solution.py:22
  115.9 0.7 fusion.19
  116.6 3.4 %collective-permute-start.6 = (f32[256,256]{0,1:T(8,128)}, f32[256,256]{0,1:T(8,128)S(1)}, u32[]{:S(2)}, u32[]{:S(2)}) collective-permute-start(f32[256,256]{0,1:T(8,128)} %get-tuple-element.20), channel_id=1, source_target_pairs={{0,1},{1,2},{2,3},{4,5},{5,6},{6,7},{8,9},{9,10},{10,11},{12,13},{... | collective-permute-start | bytes 786440 | tf_op jit(solution)/shard_map/ppermute | solution.py:21
  120.0 2.4 %collective-permute-start.7 = (f32[256,256]{0,1:T(8,128)S(1)}, f32[256,256]{0,1:T(8,128)}, u32[]{:S(2)}, u32[]{:S(2)}) collective-permute-start(f32[256,256]{0,1:T(8,128)S(1)} %get-tuple-element.19), channel_id=1, source_target_pairs={{1,0},{2,1},{3,2},{5,4},{6,5},{7,6},{9,8},{10,9},{11,10},{13,12},{... | collective-permute-start | bytes 786440 | tf_op jit(solution)/shard_map/ppermute | solution.py:22
  122.7 4.4 %collective-permute-done.6 = f32[256,256]{0,1:T(8,128)S(1)} collective-permute-done((f32[256,256]{0,1:T(8,128)}, f32[256,256]{0,1:T(8,128)S(1)}, u32[]{:S(2)}, u32[]{:S(2)}) %collective-permute-start.6) | collective-permute-done | bytes 262176 | tf_op jit(solution)/shard_map/ppermute | solution.py:21
  127.1 0.7 copy-done.7
  127.8 3.1 %collective-permute-done.7 = f32[256,256]{0,1:T(8,128)} collective-permute-done((f32[256,256]{0,1:T(8,128)S(1)}, f32[256,256]{0,1:T(8,128)}, u32[]{:S(2)}, u32[]{:S(2)}) %collective-permute-start.7) | collective-permute-done | bytes 262176 | tf_op jit(solution)/shard_map/ppermute | solution.py:22
  130.9 1.3 pad_maximum_fusion
  133.4 0.6 convolution_add_fusion.2
  135.6 1.7 %dynamic_update_slice.14 = f32[256,512]{1,0:T(8,128)S(1)} dynamic-update-slice(f32[256,512]{1,0:T(8,128)S(1)} %copy.64, f32[128,128]{1,0:T(8,128)S(1)} %bitcast_add_fusion.1, s32[]{:T(128)} %constant.24.clone.1, s32[]{:T(128)S(6)} %min.9) | dynamic-update-slice | bytes 131076 | tf_op jit(solution)/shard_map/dynamic_update_slice | solution.py:80
  137.4 0.7 copy-done.1
  138.0 1.7 %dynamic_update_slice.15 = f32[256,512]{1,0:T(8,128)} dynamic-update-slice(f32[256,512]{1,0:T(8,128)} %copy-done.1, f32[128,128]{1,0:T(8,128)S(1)} %dynamic-slice_add_fusion, s32[]{:T(128)} %constant.29.clone.1, s32[]{:T(128)S(6)} %min.10) | dynamic-update-slice | bytes 131076 | tf_op jit(solution)/shard_map/dynamic_update_slice | solution.py:80
  (56 shorter events, 11.7 us)
Async XLA Ops:
  6.5 82.8 %all-reduce.3.cloned.1.call-start = ((), (), s32[]{:S(2)}) async-start(), calls=%async_computation | async-start | bytes 2621440 | tf_op jit(solution)/shard_map/psum | solution.py:11
  6.5 38.3 %collective-permute-start = (f32[256,512]{1,0:T(8,128)}, f32[256,512]{1,0:T(8,128)S(1)}, u32[]{:S(2)}, u32[]{:S(2)}) collective-permute-start(f32[256,512]{1,0:T(8,128)} %param.3), channel_id=1, source_target_pairs={{0,4},{4,8},{8,12},{12,16},{16,20},{20,24},{24,28},{1,5},{5,9},{9,... | collective-permute-start | bytes 1572872 | tf_op jit(solution)/shard_map/ppermute | solution.py:21
  8.5 36.4 %collective-permute-start.1 = (f32[256,512]{1,0:T(8,128)}, f32[256,512]{1,0:T(8,128)S(1)}, u32[]{:S(2)}, u32[]{:S(2)}) collective-permute-start(f32[256,512]{1,0:T(8,128)} %param.3), channel_id=1, source_target_pairs={{4,0},{8,4},{12,8},{16,12},{20,16},{24,20},{28,24},{5,1},{9,5},{13... | collective-permute-start | bytes 1572872 | tf_op jit(solution)/shard_map/ppermute | solution.py:22
  29.4 1.2 copy-start.8
  30.7 13.6 %copy-start = (f32[256,512]{1,0:T(8,128)S(1)}, f32[256,512]{1,0:T(8,128)}, u32[]{:S(2)}) copy-start(f32[256,512]{1,0:T(8,128)} %param.3) | copy-start | bytes 1572868
  48.4 42.2 %collective-permute-start.2 = (f32[256,256]{0,1:T(8,128)}, f32[256,256]{0,1:T(8,128)S(1)}, u32[]{:S(2)}, u32[]{:S(2)}) collective-permute-start(f32[256,256]{0,1:T(8,128)} %get-tuple-element.26), channel_id=1, source_target_pairs={{0,1},{1,2},{2,3},{4,5},{5,6},{6,7},{8,9},{9,10},{10,11},{12,13},{... | collective-permute-start | bytes 786440 | tf_op jit(solution)/shard_map/ppermute | solution.py:21
  52.9 37.7 %collective-permute-start.3 = (f32[256,256]{0,1:T(8,128)}, f32[256,256]{0,1:T(8,128)}, u32[]{:S(2)}, u32[]{:S(2)}) collective-permute-start(f32[256,256]{0,1:T(8,128)} %get-tuple-element.25), channel_id=1, source_target_pairs={{1,0},{2,1},{3,2},{5,4},{6,5},{7,6},{9,8},{10,9},{11,10},{13,12},{... | collective-permute-start | bytes 786440 | tf_op jit(solution)/shard_map/ppermute | solution.py:22
  55.0 40.0 %copy-start.5 = (f32[1,128,128]{2,0,1:T(1,128)}, f32[1,128,128]{2,0,1:T(1,128)S(1)}, u32[]{:S(2)}) copy-start(f32[1,128,128]{2,0,1:T(1,128)S(1)} %get-tuple-element.30) | copy-start | bytes 196612
  55.0 41.8 %copy-start.3 = (f32[1,128,128]{2,0,1:T(1,128)}, f32[1,128,128]{2,0,1:T(1,128)S(1)}, u32[]{:S(2)}) copy-start(f32[1,128,128]{2,0,1:T(1,128)S(1)} %get-tuple-element.29) | copy-start | bytes 196612
  89.3 1.3 copy-start.2
  98.1 10.5 %collective-permute-start.4 = (f32[256,512]{1,0:T(8,128)S(1)}, f32[256,512]{1,0:T(8,128)S(1)}, u32[]{:S(2)}, u32[]{:S(2)}) collective-permute-start(f32[256,512]{1,0:T(8,128)S(1)} %dynamic_update_slice.13), channel_id=1, source_target_pairs={{0,4},{4,8},{8,12},{12,16},{16,20},{20,24},{24,28},{1,5},{5,9},{9,... | collective-permute-start | bytes 1572872 | tf_op jit(solution)/shard_map/ppermute | solution.py:21
  100.0 13.2 %collective-permute-start.5 = (f32[256,512]{1,0:T(8,128)S(1)}, f32[256,512]{1,0:T(8,128)S(1)}, u32[]{:S(2)}, u32[]{:S(2)}) collective-permute-start(f32[256,512]{1,0:T(8,128)S(1)} %dynamic_update_slice.13), channel_id=1, source_target_pairs={{4,0},{8,4},{12,8},{16,12},{20,16},{24,20},{28,24},{5,1},{9,5},{13... | collective-permute-start | bytes 1572872 | tf_op jit(solution)/shard_map/ppermute | solution.py:22
  116.6 10.5 %collective-permute-start.6 = (f32[256,256]{0,1:T(8,128)}, f32[256,256]{0,1:T(8,128)S(1)}, u32[]{:S(2)}, u32[]{:S(2)}) collective-permute-start(f32[256,256]{0,1:T(8,128)} %get-tuple-element.20), channel_id=1, source_target_pairs={{0,1},{1,2},{2,3},{4,5},{5,6},{6,7},{8,9},{9,10},{10,11},{12,13},{... | collective-permute-start | bytes 786440 | tf_op jit(solution)/shard_map/ppermute | solution.py:21
  120.0 10.9 %collective-permute-start.7 = (f32[256,256]{0,1:T(8,128)S(1)}, f32[256,256]{0,1:T(8,128)}, u32[]{:S(2)}, u32[]{:S(2)}) collective-permute-start(f32[256,256]{0,1:T(8,128)S(1)} %get-tuple-element.19), channel_id=1, source_target_pairs={{1,0},{2,1},{3,2},{5,4},{6,5},{7,6},{9,8},{10,9},{11,10},{13,12},{... | collective-permute-start | bytes 786440 | tf_op jit(solution)/shard_map/ppermute | solution.py:22
  127.1 0.7 copy-start.7
  134.6 0.8 copy-start.6
  134.6 2.6 %copy-start.4 = (f32[1,128,128]{2,0,1:T(1,128)S(1)}, f32[1,128,128]{2,0,1:T(1,128)}, u32[]{:S(2)}) copy-start(f32[1,128,128]{2,0,1:T(1,128)} %copy-done.3) | copy-start | bytes 196612
  137.2 0.8 copy-start.1
Sparse Core Ops, SparseCore 0:
  30.8 58.4 all-reduce.2
where the time goes:
time: 147 us
  waiting for transfers between devices  50.3 us (34%)
  blocking collectives  29.7 us (20%)
  starting transfers between devices  23.5 us (16%)
  between operations  14 us (10%)
  local copies, waits for them, and re-layouts  12.7 us (9%)
  matrix products  11.9 us (8%)
  other arithmetic  4.44 us (3%)
    psum x1, waiting for transfers between devices, from_root(): return lax.psum(block, axis)  34 us
    all_gather x1, blocking collectives, body(): lax.all_gather(dynamics, 'col', axis=2, tiled=True)  16.4 us
    all_gather x1, blocking collectives, body(): lax.all_gather(noise_factor, 'col', axis=1, tiled=True)  13.3 us
    ppermute x4, starting transfers between devices, extended_2(): after = lax.ppermute(leading, axis, down)  11.8 us
    ppermute x4, starting transfers between devices, extended_2(): before = lax.ppermute(last, axis, up)  11.7 us
    ppermute x4, waiting for transfers between devices, extended_2(): before = lax.ppermute(last, axis, up)  8.56 us
    ppermute x4, waiting for transfers between devices, extended_2(): after = lax.ppermute(leading, axis, down)  7.68 us
    dynamic_update_slice x4, local copies, waits for them, and re-layouts, body(): lax.dynamic_update_slice(result, updated, (jnp.int32(local * band), safe))  6.13 us
  transfers between devices with their start and end apart: 9, of which 5 were waited for; matrix products, arithmetic and copies ran while one was open for 6% of the time, Pallas kernels for 0%

commit v1 on v0

v1 whole, which is shorter than its diff:
```python
import functools

import jax
import jax.numpy as jnp
from jax import lax
from jax.experimental import pallas as pl
from jax.experimental.pallas import tpu as pltpu
from jax.sharding import PartitionSpec as P

STEPS = 2
MESH = pl.DeviceIdType.MESH
F32 = jnp.float32
BF16 = jnp.bfloat16


def split(value):
    hi = value.astype(BF16)
    return hi, (value - hi.astype(F32)).astype(BF16)


def product(a, b, transposed):
    dims = (((1,), (1,)), ((), ())) if transposed else (((1,), (0,)), ((), ()))
    dot = functools.partial(lax.dot_general, dimension_numbers=dims, preferred_element_type=F32)
    return dot(a[0], b[0]) + (dot(a[0], b[1]) + dot(a[1], b[0]))


def swap_pairs(i):
    return i + ((i // 2) % 2) * (1 - 2 * (i % 2))


def kernel(
    n_rows, n_cols, cov, dyn, fac, out,
    pe, xe, drow, dcol, nbuf, arow, acol, noise, obuf,
    local_sem, out_sem, zu_s, zu_r, zd_s, zd_r, rg_s, rg_r, sb_s, sb_r, nz_s, nz_r,
    pu_s, pu_r, pd_s, pd_r, xl_s, xl_r, xr_s, xr_r,
):
    rows, cols = cov.shape
    band = rows // 2
    half = cols // 2
    r = lax.axis_index("row")
    c = lax.axis_index("col")
    k, q = r % 2, r // 2
    n_chips = n_rows // 2
    here = swap_pairs(q)
    home = swap_pairs(c)
    distance = (here - home + n_chips) % n_chips
    step_on = 1 - 2 * k
    ring_to = swap_pairs((here + step_on + n_chips) % n_chips) * 2 + k
    ahead = jnp.where(k == 0, distance, (n_chips - distance) % n_chips)
    is_home = q == c
    sibling = r + 1 - 2 * k
    up = (r + n_rows - 1) % n_rows
    down = (r + 1) % n_rows
    left = (c + n_cols - 1) % n_cols
    right = (c + 1) % n_cols
    pending = []

    def put(cond, src, dst, send_sem, recv_sem, to):
        def make():
            return pltpu.make_async_remote_copy(
                src_ref=src, dst_ref=dst, send_sem=send_sem, recv_sem=recv_sem,
                device_id=to, device_id_type=MESH)

        @pl.when(cond)
        def _():
            make().start()

        pending.append((cond, make))

    def arrive(cond, dst, send_sem, recv_sem):
        @pl.when(cond)
        def _():
            pltpu.make_async_remote_copy(
                src_ref=dst, dst_ref=dst, send_sem=send_sem, recv_sem=recv_sem,
                device_id=(sibling, c), device_id_type=MESH).wait_recv()

    own = [pltpu.make_async_copy(cov.at[:, pl.ds(h * half, half)], pe.at[0, h, 1], local_sem.at[h]) for h in range(2)]
    own_dyn = pltpu.make_async_copy(dyn, drow.at[c], local_sem.at[2])
    own_fac = pltpu.make_async_copy(fac, nbuf.at[c], local_sem.at[3])
    for copy in (own_dyn, own_fac, own[0], own[1]):
        copy.start()

    barrier = pltpu.get_barrier_semaphore()
    for i in range(1, n_rows):
        pl.semaphore_signal(barrier, inc=1, device_id=((r + i) % n_rows, c), device_id_type=MESH)
    for i in range(1, n_cols):
        pl.semaphore_signal(barrier, inc=1, device_id=(r, (c + i) % n_cols), device_id_type=MESH)
    pl.semaphore_wait(barrier, n_rows + n_cols - 2)

    not_first, not_last = r > 0, r < n_rows - 1
    has_left, has_right = c > 0, c < n_cols - 1

    def send_half(step, h):
        src = cov.at[:, pl.ds(h * half, half)] if step == 0 else pe.at[step, h, 1]
        put(not_last, src, pe.at[step, h, 0], pd_s.at[step, h], pd_r.at[step, h], (down, c))
        put(not_first, src, pe.at[step, h, 2], pu_s.at[step, h], pu_r.at[step, h], (up, c))

    def to_plane(shard, src):
        put(is_home, src, dcol.at[k, shard], rg_s.at[shard], rg_r.at[shard], (ring_to, c))
        put(is_home, src, dcol.at[k, shard], sb_s.at[0, shard], sb_r.at[k, shard], (sibling, c))

    def ring_relay(cond, shard):
        cond = jnp.logical_and(cond, jnp.logical_not(is_home))
        block = dcol.at[k, shard]
        arrive(cond, block, rg_s.at[shard], rg_r.at[shard])
        put(jnp.logical_and(cond, ahead < n_chips - 1), block, block, rg_s.at[shard], rg_r.at[shard], (ring_to, c))
        put(cond, block, block, sb_s.at[1, shard], sb_r.at[k, shard], (sibling, c))

    put(has_right, dyn, drow.at[c], zu_s.at[c], zu_r.at[c], (r, right))
    put(has_left, dyn, drow.at[c], zd_s.at[c], zd_r.at[c], (r, left))
    to_plane(c, dyn)
    put(jnp.logical_not(is_home), fac, nbuf.at[c], nz_s, nz_r.at[c], (r, q))
    send_half(0, 0)
    send_half(0, 1)

    for step in range(STEPS):
        @pl.when(jnp.logical_not(not_first))
        def _():
            for h in range(2):
                pe[step, h, 0] = jnp.zeros((rows, half), F32)

        @pl.when(jnp.logical_not(not_last))
        def _():
            for h in range(2):
                pe[step, h, 2] = jnp.zeros((rows, half), F32)

        @pl.when(jnp.logical_not(has_left))
        def _():
            xe[step, 0] = jnp.zeros((rows, half), F32)

        @pl.when(jnp.logical_not(has_right))
        def _():
            xe[step, 3] = jnp.zeros((rows, half), F32)

    zero = jnp.zeros((band, band), BF16)
    for part in range(2):
        arow[part, 0, band:, :band] = zero
        arow[part, 2, :band, band:] = zero
        for j in range(2):
            acol[j, part, 0, band:, :band] = zero
            acol[j, part, 2, :band, band:] = zero
    noise[...] = jnp.zeros_like(noise)

    def column_hop(s):
        shard_up = jnp.maximum(c - s, 0)
        shard_down = jnp.minimum(c + s, n_cols - 1)
        from_left, from_right = c - s >= 0, c + s < n_cols
        block = drow.at[shard_up]
        arrive(from_left, block, zu_s.at[shard_up], zu_r.at[shard_up])
        put(jnp.logical_and(from_left, has_right), block, block, zu_s.at[shard_up], zu_r.at[shard_up], (r, right))
        other = drow.at[shard_down]
        arrive(from_right, other, zd_s.at[shard_down], zd_r.at[shard_down])
        put(jnp.logical_and(from_right, has_left), other, other, zd_s.at[shard_down], zd_r.at[shard_down], (r, left))
        for cond, shard in ((from_left, shard_up), (from_right, shard_down)):
            go = jnp.logical_and(cond, is_home)
            src = drow.at[shard]
            put(go, src, dcol.at[k, shard], rg_s.at[shard], rg_r.at[shard], (ring_to, c))
            put(go, src, dcol.at[k, shard], sb_s.at[0, shard], sb_r.at[k, shard], (sibling, c))

    def plane_hop(s):
        if s == 0:
            ring_relay(r >= 0, c)
        else:
            ring_relay(c - s >= 0, jnp.maximum(c - s, 0))
            ring_relay(c + s < n_cols, jnp.minimum(c + s, n_cols - 1))

    for s in range(1, n_cols):
        column_hop(s)
        plane_hop(s - 1)
    own_dyn.wait()

    def assemble(source, target):
        def block(i, o):
            return source[:, i, o].reshape(band, band)

        for i in range(2):
            for o in range(5):
                at = i + o
                hi, lo = split(block(i, o))
                span = pl.ds((at % 2) * band, band)
                target[0, at // 2, i * band:(i + 1) * band, span] = hi
                target[1, at // 2, i * band:(i + 1) * band, span] = lo

    assemble(drow, arow)
    own[0].wait()
    own[1].wait()

    def first_half(step, h):
        total = product((arow[0, 1], arow[1, 1]), split(pe[step, h, 1]), False)
        arrive(not_first, pe.at[step, h, 0], pd_s.at[step, h], pd_r.at[step, h])
        total += product((arow[0, 0], arow[1, 0]), split(pe[step, h, 0]), False)
        arrive(not_last, pe.at[step, h, 2], pu_s.at[step, h], pu_r.at[step, h])
        total += product((arow[0, 2], arow[1, 2]), split(pe[step, h, 2]), False)
        xe[step, 1 + h] = total
        if h == 0:
            put(has_left, xe.at[step, 1], xe.at[step, 3], xl_s.at[step], xl_r.at[step], (r, left))
        else:
            put(has_right, xe.at[step, 2], xe.at[step, 0], xr_s.at[step], xr_r.at[step], (r, right))

    def second_half(step, h):
        def term(t):
            return product(split(xe[step, h + t]), (acol[h, 0, t], acol[h, 1, t]), True)

        if h == 0:
            total = term(1) + term(2) + noise[0]
            arrive(has_left, xe.at[step, 0], xr_s.at[step], xr_r.at[step])
            total += term(0)
        else:
            total = term(0) + term(1) + noise[1]
            arrive(has_right, xe.at[step, 3], xl_s.at[step], xl_r.at[step])
            total += term(2)
        if step + 1 < STEPS:
            pe[step + 1, h, 1] = total
            send_half(step + 1, h)
        else:
            obuf[h] = total
            pltpu.make_async_copy(obuf.at[h], out.at[:, pl.ds(h * half, half)], out_sem.at[h]).start()

    for h in range(2):
        first_half(0, h)

    own_fac.wait()
    for z in range(n_cols):
        arrive(jnp.logical_and(is_home, c != z), nbuf.at[z], nz_s, nz_r.at[z])

    @pl.when(is_home)
    def _():
        for i in range(2):
            block = nbuf[:, i].reshape(band, band)
            block = 0.5 * (block + block.T)
            noise[k, i * band:(i + 1) * band, i * band:(i + 1) * band] = block

    plane_hop(n_cols - 1)

    @pl.when(is_home)
    def _():
        acol[k] = arow[...]

    @pl.when(jnp.logical_not(is_home))
    def _():
        assemble(dcol.at[k], acol.at[k])

    for z in range(n_cols):
        arrive(r >= 0, dcol.at[1 - k, z], sb_s.at[0, z], sb_r.at[1 - k, z])
    assemble(dcol.at[1 - k], acol.at[1 - k])

    for step in range(STEPS):
        order = (1, 0) if step % 2 == 0 else (0, 1)
        if step > 0:
            for h in order[::-1]:
                first_half(step, h)
        for h in order:
            second_half(step, h)

    for h in range(2):
        pltpu.make_async_copy(obuf.at[h], out.at[:, pl.ds(h * half, half)], out_sem.at[h]).wait()
    for cond, make in pending:
        @pl.when(cond)
        def _(make=make):
            make().wait_send()


def body(n_rows, n_cols, covariance, dynamics, noise_factor):
    rows, cols = covariance.shape
    band = dynamics.shape[3]
    half = cols // 2
    dma = pltpu.SemaphoreType.DMA
    shards = (n_cols,)
    pairs = (STEPS, 2)
    return pl.pallas_call(
        functools.partial(kernel, n_rows, n_cols),
        out_shape=jax.ShapeDtypeStruct((rows, cols), F32),
        in_specs=[pl.BlockSpec(memory_space=pl.ANY)] * 3,
        out_specs=pl.BlockSpec(memory_space=pl.ANY),
        scratch_shapes=[
            pltpu.VMEM((STEPS, 2, 3, rows, half), F32),
            pltpu.VMEM((STEPS, 4, rows, half), F32),
            pltpu.VMEM((n_cols,) + dynamics.shape, F32),
            pltpu.VMEM((2, n_cols) + dynamics.shape, F32),
            pltpu.VMEM((n_cols,) + noise_factor.shape, F32),
            pltpu.VMEM((2, 3, rows, rows), BF16),
            pltpu.VMEM((2, 2, 3, rows, rows), BF16),
            pltpu.VMEM((2, rows, half), F32),
            pltpu.VMEM((2, rows, half), F32),
            dma((4,)), dma((2,)),
            dma(shards), dma(shards), dma(shards), dma(shards),
            dma(shards), dma(shards), dma((2,) + shards), dma((2,) + shards),
            dma, dma(shards),
            dma(pairs), dma(pairs), dma(pairs), dma(pairs),
            dma((STEPS,)), dma((STEPS,)), dma((STEPS,)), dma((STEPS,)),
        ],
        compiler_params=pltpu.CompilerParams(
            collective_id=0, has_side_effects=True, vmem_limit_bytes=40 * 1024 * 1024),
    )(covariance, dynamics, noise_factor)


def solution(mesh):
    in_specs = (P("row", "col"), P("row", None, "col", None), P("row", "col", None))
    out_specs = P("row", "col")
    run = functools.partial(body, mesh.shape["row"], mesh.shape["col"])
    return jax.shard_map(run, mesh=mesh, in_specs=in_specs, out_specs=out_specs, check_vma=False)
```

time: 147 us -> 60.7 us (0.41)
  the two profiles are of different devices: /device:TPU:18 before, /device:TPU:20 now
where the time goes in v1:
time: 60.7 us; the launch traced here: 60.5 us
  Pallas kernels  57 us (94%)
  local copies, waits for them, and re-layouts  3.51 us (6%)
    pallas_call x1, Pallas kernels, body(): pl.pallas_call(functools.partial(kernel, n_rows, n_cols), out_shape=jax.S...  57 us
    unnamed x7, local copies, waits for them, and re-layouts  3.51 us

profile of v1, /device:TPU:20, one launch (start us, length us, event | category | flops | bytes accessed | tf_op | source)
XLA Modules:
  0.0 60.5 jit_solution(1424383050044550554)
XLA Ops:
  0.0 0.0 copy-start
  0.0 1.0 %copy-done = f32[256,512]{1,0:T(8,128)S(1)} copy-done((f32[256,512]{1,0:T(8,128)S(1)}, f32[256,512]{1,0:T(8,128)}, u32[]{:S(2)}) %copy-start) | copy-done | bytes 524312
  1.0 0.0 copy-start.1
  1.0 0.9 %copy-done.1 = f32[2,5,32,128]{3,2,1,0:T(8,128)S(1)} copy-done((f32[2,5,32,128]{3,2,1,0:T(8,128)S(1)}, f32[2,5,32,128]{3,2,1,0:T(8,128)}, u32[]{:S(2)}) %copy-start.1) | copy-done | bytes 163864
  2.0 0.0 copy-start.2
  2.0 0.8 %copy-done.2 = f32[2,32,128]{2,1,0:T(8,128)S(1)} copy-done((f32[2,32,128]{2,1,0:T(8,128)S(1)}, f32[2,32,128]{2,1,0:T(8,128)}, u32[]{:S(2)}) %copy-start.2) | copy-done | bytes 32792
  2.7 57.0 %shard_map.37 = f32[256,512]{1,0:T(8,128)S(1)} custom-call(f32[256,512]{1,0:T(8,128)S(1)} %copy-done, f32[2,5,32,128]{3,2,1,0:T(8,128)S(1)} %copy-done.1, f32[2,32,128]{2,1,0:T(8,128)S(1)} %copy-done.2), custom_call_target="tpu_custom_call" | custom-call | tf_op jit(solution)/shard_map/pallas_call | solution.py:270
  59.7 0.8 %copy.5 = f32[256,512]{1,0:T(8,128)} copy(f32[256,512]{1,0:T(8,128)S(1)} %shard_map.37) | data formatting | bytes 1048576
Async XLA Ops:
  0.0 1.0 %copy-start = (f32[256,512]{1,0:T(8,128)S(1)}, f32[256,512]{1,0:T(8,128)}, u32[]{:S(2)}) copy-start(f32[256,512]{1,0:T(8,128)} %cov.1) | copy-start | bytes 1572868
  1.0 0.9 %copy-start.1 = (f32[2,5,32,128]{3,2,1,0:T(8,128)S(1)}, f32[2,5,32,128]{3,2,1,0:T(8,128)}, u32[]{:S(2)}) copy-start(f32[2,5,32,128]{3,2,1,0:T(8,128)} %dyn.1) | copy-start | bytes 491524
  2.0 0.8 %copy-start.2 = (f32[2,32,128]{2,1,0:T(8,128)S(1)}, f32[2,32,128]{2,1,0:T(8,128)}, u32[]{:S(2)}) copy-start(f32[2,32,128]{2,1,0:T(8,128)} %fac.1) | copy-start | bytes 98308

commit v2 on v1

--- a/solution.py
+++ b/solution.py
@@ -95,20 +95,23 @@
         put(not_last, src, pe.at[step, h, 0], pd_s.at[step, h], pd_r.at[step, h], (down, c))
         put(not_first, src, pe.at[step, h, 2], pu_s.at[step, h], pu_r.at[step, h], (up, c))
 
-    def to_plane(shard, src):
-        put(is_home, src, dcol.at[k, shard], rg_s.at[shard], rg_r.at[shard], (ring_to, c))
-        put(is_home, src, dcol.at[k, shard], sb_s.at[0, shard], sb_r.at[k, shard], (sibling, c))
-
-    def ring_relay(cond, shard):
-        cond = jnp.logical_and(cond, jnp.logical_not(is_home))
-        block = dcol.at[k, shard]
-        arrive(cond, block, rg_s.at[shard], rg_r.at[shard])
-        put(jnp.logical_and(cond, ahead < n_chips - 1), block, block, rg_s.at[shard], rg_r.at[shard], (ring_to, c))
-        put(cond, block, block, sb_s.at[1, shard], sb_r.at[k, shard], (sibling, c))
-
-    put(has_right, dyn, drow.at[c], zu_s.at[c], zu_r.at[c], (r, right))
-    put(has_left, dyn, drow.at[c], zd_s.at[c], zd_r.at[c], (r, left))
-    to_plane(c, dyn)
+    def to_plane(cond, z, i, src):
+        go = jnp.logical_and(cond, is_home)
+        put(go, src, dcol.at[k, z, i], rg_s.at[z, i], rg_r.at[z, i], (ring_to, c))
+        put(go, src, dcol.at[k, z, i], sb_s.at[0, z, i], sb_r.at[k, z, i], (sibling, c))
+
+    def ring_relay(cond, z, i, passes):
+        block = dcol.at[k, z, i]
+        arrive(cond, block, rg_s.at[z, i], rg_r.at[z, i])
+        if passes:
+            put(cond, block, block, rg_s.at[z, i], rg_r.at[z, i], (ring_to, c))
+        put(cond, block, block, sb_s.at[1, z, i], sb_r.at[k, z, i], (sibling, c))
+
+    for i in range(2):
+        put(has_right, dyn.at[i], drow.at[c, i], zu_s.at[c, i], zu_r.at[c, i], (r, right))
+        put(has_left, dyn.at[i], drow.at[c, i], zd_s.at[c, i], zd_r.at[c, i], (r, left))
+    for i in range(2):
+        to_plane(r >= 0, c, i, dyn.at[i])
     put(jnp.logical_not(is_home), fac, nbuf.at[c], nz_s, nz_r.at[c], (r, q))
     send_half(0, 0)
     send_half(0, 1)
@@ -141,32 +144,36 @@
             acol[j, part, 2, :band, band:] = zero
     noise[...] = jnp.zeros_like(noise)
 
-    def column_hop(s):
-        shard_up = jnp.maximum(c - s, 0)
-        shard_down = jnp.minimum(c + s, n_cols - 1)
-        from_left, from_right = c - s >= 0, c + s < n_cols
-        block = drow.at[shard_up]
-        arrive(from_left, block, zu_s.at[shard_up], zu_r.at[shard_up])
-        put(jnp.logical_and(from_left, has_right), block, block, zu_s.at[shard_up], zu_r.at[shard_up], (r, right))
-        other = drow.at[shard_down]
-        arrive(from_right, other, zd_s.at[shard_down], zd_r.at[shard_down])
-        put(jnp.logical_and(from_right, has_left), other, other, zd_s.at[shard_down], zd_r.at[shard_down], (r, left))
-        for cond, shard in ((from_left, shard_up), (from_right, shard_down)):
-            go = jnp.logical_and(cond, is_home)
-            src = drow.at[shard]
-            put(go, src, dcol.at[k, shard], rg_s.at[shard], rg_r.at[shard], (ring_to, c))
-            put(go, src, dcol.at[k, shard], sb_s.at[0, shard], sb_r.at[k, shard], (sibling, c))
-
-    def plane_hop(s):
-        if s == 0:
-            ring_relay(r >= 0, c)
-        else:
-            ring_relay(c - s >= 0, jnp.maximum(c - s, 0))
-            ring_relay(c + s < n_cols, jnp.minimum(c + s, n_cols - 1))
-
-    for s in range(1, n_cols):
-        column_hop(s)
-        plane_hop(s - 1)
+    def sources(s):
+        found = [(c - s >= 0, jnp.maximum(c - s, 0))]
+        return found if s == 0 else found + [(c + s < n_cols, jnp.minimum(c + s, n_cols - 1))]
+
+    def column_hop(s, i):
+        (from_left, low), (from_right, high) = sources(s)
+        block = drow.at[low, i]
+        arrive(from_left, block, zu_s.at[low, i], zu_r.at[low, i])
+        put(jnp.logical_and(from_left, has_right), block, block, zu_s.at[low, i], zu_r.at[low, i], (r, right))
+        other = drow.at[high, i]
+        arrive(from_right, other, zd_s.at[high, i], zd_r.at[high, i])
+        put(jnp.logical_and(from_right, has_left), other, other, zd_s.at[high, i], zd_r.at[high, i], (r, left))
+        to_plane(from_left, low, i, block)
+        to_plane(from_right, high, i, other)
+
+    def plane_hop(event, who, passes=True):
+        for cond, z in sources(event // 2):
+            ring_relay(jnp.logical_and(cond, who), z, event % 2, passes)
+
+    n_events = 2 * n_cols
+    leaf = ahead == n_chips - 1
+    near = jnp.logical_and(ahead == 1, jnp.logical_not(leaf))
+    far = jnp.logical_and(ahead > 1, jnp.logical_not(leaf))
+    near_lag, far_lag = 2, 4
+    for event in range(2, n_events):
+        column_hop(event // 2, event % 2)
+        if event >= near_lag:
+            plane_hop(event - near_lag, near)
+        if event >= far_lag:
+            plane_hop(event - far_lag, far)
     own_dyn.wait()
 
     def assemble(source, target):
@@ -216,8 +223,12 @@
             obuf[h] = total
             pltpu.make_async_copy(obuf.at[h], out.at[:, pl.ds(h * half, half)], out_sem.at[h]).start()
 
-    for h in range(2):
-        first_half(0, h)
+    for event in range(n_events - near_lag, n_events):
+        plane_hop(event, near)
+    first_half(0, 0)
+    for event in range(n_events - far_lag, n_events):
+        plane_hop(event, far)
+    first_half(0, 1)
 
     own_fac.wait()
     for z in range(n_cols):
@@ -230,7 +241,8 @@
             block = 0.5 * (block + block.T)
             noise[k, i * band:(i + 1) * band, i * band:(i + 1) * band] = block
 
-    plane_hop(n_cols - 1)
+    for event in range(n_events):
+        plane_hop(event, leaf, False)
 
     @pl.when(is_home)
     def _():
@@ -241,7 +253,8 @@
         assemble(dcol.at[k], acol.at[k])
 
     for z in range(n_cols):
-        arrive(r >= 0, dcol.at[1 - k, z], sb_s.at[0, z], sb_r.at[1 - k, z])
+        for i in range(2):
+            arrive(r >= 0, dcol.at[1 - k, z, i], sb_s.at[0, z, i], sb_r.at[1 - k, z, i])
     assemble(dcol.at[1 - k], acol.at[1 - k])
 
     for step in range(STEPS):
@@ -265,13 +278,13 @@
     band = dynamics.shape[3]
     half = cols // 2
     dma = pltpu.SemaphoreType.DMA
-    shards = (n_cols,)
+    shards = (n_cols, 2)
     pairs = (STEPS, 2)
     return pl.pallas_call(
         functools.partial(kernel, n_rows, n_cols),
         out_shape=jax.ShapeDtypeStruct((rows, cols), F32),
-        in_specs=[pl.BlockSpec(memory_space=pl.ANY)] * 3,
-        out_specs=pl.BlockSpec(memory_space=pl.ANY),
+        in_specs=[pl.BlockSpec(memory_space=pltpu.HBM)] * 3,
+        out_specs=pl.BlockSpec(memory_space=pltpu.HBM),
         scratch_shapes=[
             pltpu.VMEM((STEPS, 2, 3, rows, half), F32),
             pltpu.VMEM((STEPS, 4, rows, half), F32),
@@ -285,12 +298,12 @@
             dma((4,)), dma((2,)),
             dma(shards), dma(shards), dma(shards), dma(shards),
             dma(shards), dma(shards), dma((2,) + shards), dma((2,) + shards),
-            dma, dma(shards),
+            dma, dma((n_cols,)),
             dma(pairs), dma(pairs), dma(pairs), dma(pairs),
             dma((STEPS,)), dma((STEPS,)), dma((STEPS,)), dma((STEPS,)),
         ],
         compiler_params=pltpu.CompilerParams(
-            collective_id=0, has_side_effects=True, vmem_limit_bytes=40 * 1024 * 1024),
+            collective_id=0, has_side_effects=True, vmem_limit_bytes=62 * 1024 * 1024),
     )(covariance, dynamics, noise_factor)
 
 

time: 60.7 us -> 54.1 us (0.89)
  the two profiles are of different devices: /device:TPU:20 before, /device:TPU:19 now
where the time goes in v2:
time: 54.1 us; the launch traced here: 54 us
  Pallas kernels  52.1 us (96%)
  local copies, waits for them, and re-layouts  1.87 us (3%)
    pallas_call x1, Pallas kernels, body(): pl.pallas_call(functools.partial(kernel, n_rows, n_cols), out_shape=jax.S...  52.1 us
    unnamed x1, local copies, waits for them, and re-layouts  1.87 us

profile of v2, /device:TPU:19, one launch (start us, length us, event | category | flops | bytes accessed | tf_op | source)
XLA Modules:
  0.0 54.0 jit_solution(15471862671768527272)
XLA Ops:
  0.0 52.1 %shard_map.37 = f32[256,512]{1,0:T(8,128)} custom-call(f32[256,512]{1,0:T(8,128)} %cov.1, f32[2,5,32,128]{3,2,1,0:T(8,128)} %dyn.1, f32[2,32,128]{2,1,0:T(8,128)} %fac.1), custom_call_target="tpu_custom_call" | custom-call | tf_op jit(solution)/shard_map/pallas_call | solution.py:283
  52.1 1.9 %copy.5 = f32[256,512]{1,0:T(8,128)} copy(f32[256,512]{1,0:T(8,128)} %shard_map.37) | data formatting | bytes 1048576

commit v3 on v2

--- a/solution.py
+++ b/solution.py
@@ -30,9 +30,9 @@
 
 def kernel(
     n_rows, n_cols, cov, dyn, fac, out,
-    pe, xe, drow, dcol, nbuf, arow, acol, noise, obuf,
+    pe, xe, drow, dcol, nbuf, arow, acol, noise, obuf, rbuf,
     local_sem, out_sem, zu_s, zu_r, zd_s, zd_r, rg_s, rg_r, sb_s, sb_r, nz_s, nz_r,
-    pu_s, pu_r, pd_s, pd_r, xl_s, xl_r, xr_s, xr_r,
+    pu_s, pu_r, pd_s, pd_r, xl_s, xl_r, xr_s, xr_r, rl_s, rl_r,
 ):
     rows, cols = cov.shape
     band = rows // 2
@@ -90,10 +90,36 @@
     not_first, not_last = r > 0, r < n_rows - 1
     has_left, has_right = c > 0, c < n_cols - 1
 
+    quarter = half // 2
+
+    def columns(j):
+        return pl.ds(j * quarter, quarter)
+
+    detour = n_chips == 4
+    upper, lower, last = n_rows // 2 - 1, n_rows // 2, n_rows - 1
+    via_down, via_up = last, 0
+
     def send_half(step, h):
-        src = cov.at[:, pl.ds(h * half, half)] if step == 0 else pe.at[step, h, 1]
-        put(not_last, src, pe.at[step, h, 0], pd_s.at[step, h], pd_r.at[step, h], (down, c))
-        put(not_first, src, pe.at[step, h, 2], pu_s.at[step, h], pu_r.at[step, h], (up, c))
+        for j in range(2):
+            n = 2 * h + j
+            src = cov.at[:, columns(n)] if step == 0 else pe.at[step, h, 1, :, columns(j)]
+            goes_down, goes_up = not_last, not_first
+            if detour and j == 1:
+                goes_down = jnp.logical_and(not_last, r != upper)
+                goes_up = jnp.logical_and(not_first, r != lower)
+                block = rbuf.at[step, h]
+                put(r == upper, src, block, rl_s.at[step, h], rl_r.at[step, h], (via_down, c))
+                put(r == lower, src, block, rl_s.at[step, h], rl_r.at[step, h], (via_up, c))
+            put(goes_down, src, pe.at[step, h, 0, :, columns(j)], pd_s.at[step, n], pd_r.at[step, n], (down, c))
+            put(goes_up, src, pe.at[step, h, 2, :, columns(j)], pu_s.at[step, n], pu_r.at[step, n], (up, c))
+
+    def relay_half(step, h):
+        if not detour:
+            return
+        n, at, block = 2 * h + 1, columns(1), rbuf.at[step, h]
+        arrive(jnp.logical_or(r == via_down, r == via_up), block, rl_s.at[step, h], rl_r.at[step, h])
+        put(r == via_down, block, pe.at[step, h, 0, :, at], pd_s.at[step, n], pd_r.at[step, n], (lower, c))
+        put(r == via_up, block, pe.at[step, h, 2, :, at], pu_s.at[step, n], pu_r.at[step, n], (upper, c))
 
     def to_plane(cond, z, i, src):
         go = jnp.logical_and(cond, is_home)
@@ -167,9 +193,11 @@
     leaf = ahead == n_chips - 1
     near = jnp.logical_and(ahead == 1, jnp.logical_not(leaf))
     far = jnp.logical_and(ahead > 1, jnp.logical_not(leaf))
-    near_lag, far_lag = 2, 4
+    near_lag, far_lag = 5, 8
     for event in range(2, n_events):
         column_hop(event // 2, event % 2)
+        if event in (n_events - 3, n_events - 1):
+            relay_half(0, (event - n_events + 3) // 2)
         if event >= near_lag:
             plane_hop(event - near_lag, near)
         if event >= far_lag:
@@ -193,16 +221,22 @@
     own[1].wait()
 
     def first_half(step, h):
-        total = product((arow[0, 1], arow[1, 1]), split(pe[step, h, 1]), False)
-        arrive(not_first, pe.at[step, h, 0], pd_s.at[step, h], pd_r.at[step, h])
-        total += product((arow[0, 0], arow[1, 0]), split(pe[step, h, 0]), False)
-        arrive(not_last, pe.at[step, h, 2], pu_s.at[step, h], pu_r.at[step, h])
-        total += product((arow[0, 2], arow[1, 2]), split(pe[step, h, 2]), False)
-        xe[step, 1 + h] = total
-        if h == 0:
-            put(has_left, xe.at[step, 1], xe.at[step, 3], xl_s.at[step], xl_r.at[step], (r, left))
-        else:
-            put(has_right, xe.at[step, 2], xe.at[step, 0], xr_s.at[step], xr_r.at[step], (r, right))
+        inner = product((arow[0, 1], arow[1, 1]), split(pe[step, h, 1]), False)
+        for j in range(2):
+            n, at = 2 * h + j, columns(j)
+            if step > 0 and j == 1:
+                relay_half(step, h)
+            total = inner[:, j * quarter:(j + 1) * quarter]
+            arrive(not_first, pe.at[step, h, 0, :, at], pd_s.at[step, n], pd_r.at[step, n])
+            total += product((arow[0, 0], arow[1, 0]), split(pe[step, h, 0, :, at]), False)
+            arrive(not_last, pe.at[step, h, 2, :, at], pu_s.at[step, n], pu_r.at[step, n])
+            total += product((arow[0, 2], arow[1, 2]), split(pe[step, h, 2, :, at]), False)
+            xe[step, 1 + h, :, at] = total
+            src = xe.at[step, 1 + h, :, at]
+            if h == 0:
+                put(has_left, src, xe.at[step, 3, :, at], xl_s.at[step, j], xl_r.at[step, j], (r, left))
+            else:
+                put(has_right, src, xe.at[step, 0, :, at], xr_s.at[step, j], xr_r.at[step, j], (r, right))
 
     def second_half(step, h):
         def term(t):
@@ -210,11 +244,13 @@
 
         if h == 0:
             total = term(1) + term(2) + noise[0]
-            arrive(has_left, xe.at[step, 0], xr_s.at[step], xr_r.at[step])
+            for j in range(2):
+                arrive(has_left, xe.at[step, 0, :, columns(j)], xr_s.at[step, j], xr_r.at[step, j])
             total += term(0)
         else:
             total = term(0) + term(1) + noise[1]
-            arrive(has_right, xe.at[step, 3], xl_s.at[step], xl_r.at[step])
+            for j in range(2):
+                arrive(has_right, xe.at[step, 3, :, columns(j)], xl_s.at[step, j], xl_r.at[step, j])
             total += term(2)
         if step + 1 < STEPS:
             pe[step + 1, h, 1] = total
@@ -280,6 +316,7 @@
     dma = pltpu.SemaphoreType.DMA
     shards = (n_cols, 2)
     pairs = (STEPS, 2)
+    quarters = (STEPS, 4)
     return pl.pallas_call(
         functools.partial(kernel, n_rows, n_cols),
         out_shape=jax.ShapeDtypeStruct((rows, cols), F32),
@@ -295,12 +332,13 @@
             pltpu.VMEM((2, 2, 3, rows, rows), BF16),
             pltpu.VMEM((2, rows, half), F32),
             pltpu.VMEM((2, rows, half), F32),
+            pltpu.VMEM((STEPS, 2, rows, half // 2), F32),
             dma((4,)), dma((2,)),
             dma(shards), dma(shards), dma(shards), dma(shards),
             dma(shards), dma(shards), dma((2,) + shards), dma((2,) + shards),
             dma, dma((n_cols,)),
-            dma(pairs), dma(pairs), dma(pairs), dma(pairs),
-            dma((STEPS,)), dma((STEPS,)), dma((STEPS,)), dma((STEPS,)),
+            dma(quarters), dma(quarters), dma(quarters), dma(quarters),
+            dma(pairs), dma(pairs), dma(pairs), dma(pairs), dma(pairs), dma(pairs),
         ],
         compiler_params=pltpu.CompilerParams(
             collective_id=0, has_side_effects=True, vmem_limit_bytes=62 * 1024 * 1024),

time: 54.1 us -> 49.2 us (0.909)
  the two profiles are of different devices: /device:TPU:19 before, /device:TPU:12 now
where the time goes in v3:
time: 49.2 us; the launch traced here: 49 us
  Pallas kernels  47.1 us (96%)
  local copies, waits for them, and re-layouts  1.87 us (4%)
    pallas_call x1, Pallas kernels, body(): pl.pallas_call(functools.partial(kernel, n_rows, n_cols), out_shape=jax.S...  47.1 us
    unnamed x1, local copies, waits for them, and re-layouts  1.87 us

profile of v3, /device:TPU:12, one launch (start us, length us, event | category | flops | bytes accessed | tf_op | source)
XLA Modules:
  0.0 49.0 jit_solution(11117775967131784165)
XLA Ops:
  0.0 47.1 %shard_map.37 = f32[256,512]{1,0:T(8,128)} custom-call(f32[256,512]{1,0:T(8,128)} %cov.1, f32[2,5,32,128]{3,2,1,0:T(8,128)} %dyn.1, f32[2,32,128]{2,1,0:T(8,128)} %fac.1), custom_call_target="tpu_custom_call" | custom-call | tf_op jit(solution)/shard_map/pallas_call | solution.py:320
  47.1 1.9 %copy.5 = f32[256,512]{1,0:T(8,128)} copy(f32[256,512]{1,0:T(8,128)} %shard_map.37) | data formatting | bytes 1048576

commit v4 on v3

--- a/solution.py
+++ b/solution.py
@@ -293,20 +293,26 @@
             arrive(r >= 0, dcol.at[1 - k, z, i], sb_s.at[0, z, i], sb_r.at[1 - k, z, i])
     assemble(dcol.at[1 - k], acol.at[1 - k])
 
+    def drain(sends):
+        for cond, make in sends:
+            @pl.when(cond)
+            def _(make=make):
+                make().wait_send()
+
+    early = len(pending)
     for step in range(STEPS):
         order = (1, 0) if step % 2 == 0 else (0, 1)
         if step > 0:
+            if step == 1:
+                drain(pending[:early])
             for h in order[::-1]:
                 first_half(step, h)
         for h in order:
             second_half(step, h)
 
+    drain(pending[early:])
     for h in range(2):
         pltpu.make_async_copy(obuf.at[h], out.at[:, pl.ds(h * half, half)], out_sem.at[h]).wait()
-    for cond, make in pending:
-        @pl.when(cond)
-        def _(make=make):
-            make().wait_send()
 
 
 def body(n_rows, n_cols, covariance, dynamics, noise_factor):

time: 49.2 us -> 48.9 us (level)
  no operation moved by 1% of the time
where the time goes in v4:
time: 48.9 us; the launch traced here: 48.8 us
  Pallas kernels  46.9 us (96%)
  local copies, waits for them, and re-layouts  1.87 us (4%)
    pallas_call x1, Pallas kernels, body(): pl.pallas_call(functools.partial(kernel, n_rows, n_cols), out_shape=jax.S...  46.9 us
    unnamed x1, local copies, waits for them, and re-layouts  1.87 us

profile of v4, /device:TPU:12, one launch (start us, length us, event | category | flops | bytes accessed | tf_op | source)
XLA Modules:
  0.0 48.8 jit_solution(12224784612131226120)
XLA Ops:
  0.0 46.9 %shard_map.37 = f32[256,512]{1,0:T(8,128)} custom-call(f32[256,512]{1,0:T(8,128)} %cov.1, f32[2,5,32,128]{3,2,1,0:T(8,128)} %dyn.1, f32[2,32,128]{2,1,0:T(8,128)} %fac.1), custom_call_target="tpu_custom_call" | custom-call | tf_op jit(solution)/shard_map/pallas_call | solution.py:326
  46.9 1.9 %copy.5 = f32[256,512]{1,0:T(8,128)} copy(f32[256,512]{1,0:T(8,128)} %shard_map.37) | data formatting | bytes 1048576
